TPU v7x, 512 devices: a whole 4x8x8 slice. The times are simulated.
512 devices in a mesh: grp: 16 (over z, core), vox: 32 (over x, y).
Axes of the slice: x: 4, y: 8, z: 8, core: 2. Of those that a mesh axis runs over, the one named last changes fastest.
Arguments:
- log_modulus: float32 [384, 262144], P('grp', 'vox'), may hold values from -3 to 3
- basis: bfloat16 [1024, 128], replicated, may hold values from -0.1875 to 0.1875
- sensitivity: bfloat16 [32768, 128], P('vox'), may hold values from -0.5 to 0.5
- obs_block: int32 [32768, 1], P('vox'), may hold values from 0 to 255; in each aligned block of 1024 rows (0 to 1023, 1024 to 2047, ...) at most 8 rows name the same one
- observed: float32 [32768], P('vox'), may hold values from -9 to 9
- noise_scale: float32 [32768], P('vox'), may hold values from 0.5 to 2
- perturbation: float32 [384, 32768], P('grp', 'vox'), may hold values from -6 to 6
Outputs:
- updated: float32 [384, 262144], P('grp', 'vox')
Inputs may be any that keep to these rules, and one draw needn't show every extreme that they name: `obs_block`: among the observations of one index of vox (aligned blocks of 1024 rows), no voxel block is read by more than 8 of them, and in every draw some block is read by exactly 8.
All inputs are finite; a program needn't handle non-finite values.
Results may differ from a plain program's by a relative error of at most 0.011.
Values may be sent and summed in bfloat16 or wider, within the bound.
A program may use at most 64 MiB of HBM per device.

v0:
```python
import functools
import math

import jax
import jax.numpy as jnp
from jax import lax
from jax.experimental import pallas as pl
from jax.experimental.pallas import tpu as pltpu
from jax.sharding import PartitionSpec as P

MESH = pl.DeviceIdType.MESH
HIGHEST = lax.Precision.HIGHEST
NX, NY, NZ, NC = 4, 8, 8, 2
N_VOX, N_GRP = NX * NY, NZ * NC
SIDE = 128
PIVOTS = 4
TILE = (8, 128)


def remote(src, dst, send_sem, recv_sem, device):
    return pltpu.make_async_remote_copy(
        src_ref=src, dst_ref=dst, send_sem=send_sem, recv_sem=recv_sem,
        device_id=device, device_id_type=MESH,
    )


def exchange_kernel(
    lm_ref, basis_ref, sens_ref, blk_ref, obs_ref, noise_ref, pert_ref,
    gram_ref, cross_ref, damp_ref,
    fbuf, sens_t, pred, dbuf, mbuf, sbuf, part, rbuf, tot, gbuf,
    xs_sem, xr_sem, ys_sem, yr_sem,
    ds_sem, dr_sem, ms_sem, mr_sem, dps_sem, dpr_sem, mps_sem, mpr_sem,
    rs_sem, rr_sem, as_sem, ar_sem, gs_sem, gr_sem, gps_sem, gpr_sem,
):
    g = lax.axis_index("grp")
    v = lax.axis_index("vox")
    z, core = g // NC, g % NC
    x, y = v // NY, v % NY
    partner = z * NC + (1 - core)
    j_dev, vox_dev = lm_ref.shape
    block_vox, width = basis_ref.shape
    blocks_dev = vox_dev // block_vox
    n_obs = sens_ref.shape[0]
    half = n_obs // 2
    members = j_dev * N_GRP
    scale_root = math.sqrt(members - 1)

    barrier = pltpu.get_barrier_semaphore()

    def greet_vox(i, _):
        pl.semaphore_signal(barrier, inc=1, device_id={"vox": (v + i) % N_VOX}, device_id_type=MESH)
        return 0

    def z_peer(i):
        return ((z + i) % NZ) * NC + core

    def greet_grp(i, _):
        pl.semaphore_signal(barrier, inc=1, device_id={"grp": z_peer(i)}, device_id_type=MESH)
        return 0

    lax.fori_loop(1, N_VOX, greet_vox, 0)
    lax.fori_loop(1, NZ, greet_grp, 0)
    pl.semaphore_signal(barrier, inc=1, device_id={"grp": partner}, device_id_type=MESH)

    lm = lm_ref[...]
    compliance = jnp.exp(-lm)
    stacked = jnp.concatenate(
        [compliance[:, b * block_vox : (b + 1) * block_vox] for b in range(blocks_dev)], axis=0
    ).astype(jnp.bfloat16)
    features = jnp.dot(stacked, basis_ref[...], preferred_element_type=jnp.float32)
    fbuf[y, x] = features.astype(jnp.bfloat16)
    pl.semaphore_wait(barrier, N_VOX - 1 + NZ - 1 + 1)

    def x_copy(i):
        src = (x + NX - i) % NX
        mine = remote(fbuf.at[y, x], fbuf.at[y, x], xs_sem.at[i], xr_sem.at[i],
                      {"vox": ((x + i) % NX) * NY + y})
        theirs = remote(fbuf.at[y, src], fbuf.at[y, src], xs_sem.at[i], xr_sem.at[i],
                        {"vox": ((x + i) % NX) * NY + y})
        return mine, theirs

    def y_copy(way, step, xi, arriving):
        turn = 1 if way == 0 else NY - 1
        xs = (x + xi) % NX
        back = step if arriving else step - 1
        ys = (y + (NY - turn) * back) % NY
        slot = fbuf.at[ys, xs]
        return remote(slot, slot, ys_sem.at[way, step - 1, xi], yr_sem.at[way, step - 1, xi],
                      {"vox": x * NY + (y + turn) % NY}), ys, xs

    def y_send(way, step, xi):
        y_copy(way, step, xi, False)[0].start()

    for i in (1, NX - 1, 2):
        x_copy(i)[0].start()
    y_send(0, 1, 0)
    y_send(1, 1, 0)
    sens_t[...] = sens_ref[...].T
    pred[...] = jnp.zeros_like(pred)
    blk = blk_ref[...]

    def compute(ys, xs):
        all_pred = jnp.dot(fbuf[ys, xs], sens_t[...], preferred_element_type=jnp.float32)
        first = (xs * NY + ys) * blocks_dev
        acc = pred[...]
        for b in range(blocks_dev):
            acc = jnp.where(blk == first + b, all_pred[b * j_dev : (b + 1) * j_dev], acc)
        pred[...] = acc

    compute(y, x)

    def far(n):
        return n + n // 2 - 2 * (n // 3)

    def x_turn(n, _):
        xi = far(n)
        i = NX - xi
        x_copy(i)[1].wait_recv()
        y_send(0, 1, xi)
        y_send(1, 1, xi)
        compute(y, (x + xi) % NX)
        return 0

    lax.fori_loop(1, NX, x_turn, 0)
    last = NY // 2

    def y_turn(n, _):
        step, xi = n // NX + 1, far(n % NX)
        low = n % NX < NX // 2
        up, up_y, xs = y_copy(0, step, xi, True)
        up.wait_recv()

        @pl.when((step + 1 < last) | low)
        def _():
            y_send(0, step + 1, xi)

        down, down_y, _ = y_copy(1, step, xi, True)
        down.wait_recv()

        @pl.when((step + 1 < last) | jnp.logical_not(low))
        def _():
            y_send(1, step + 1, xi)

        compute(up_y, xs)
        compute(down_y, xs)
        return 0

    lax.fori_loop(0, (last - 1) * NX, y_turn, 0)

    def y_last(n, _):
        xi = far(n)

        @pl.when(n < NX // 2)
        def _():
            y_copy(0, last, xi, True)[0].wait_recv()

        @pl.when(n >= NX // 2)
        def _():
            y_copy(1, last, xi, True)[0].wait_recv()

        compute((y + last) % NY, (x + xi) % NX)
        return 0

    lax.fori_loop(0, NX, y_last, 0)

    own_pred = pred[...]
    own_mean = jnp.mean(own_pred, axis=0, keepdims=True)
    mbuf[g] = own_mean
    dev = own_pred - own_mean
    dbuf[g] = jnp.concatenate([dev[:, :half], dev[:, half:]], axis=0).astype(jnp.bfloat16)

    def peer_copies(i, arriving):
        slot = ((z + NZ - i) % NZ) * NC + core if arriving else g
        to = {"grp": z_peer(i)}
        return (remote(dbuf.at[slot], dbuf.at[slot], ds_sem.at[i], dr_sem.at[i], to),
                remote(mbuf.at[slot], mbuf.at[slot], ms_sem.at[i], mr_sem.at[i], to))

    def partner_copies(i, arriving):
        slot = ((z + NZ - i) % NZ) * NC + (1 - core if arriving else core)
        to = {"grp": partner}
        return (remote(dbuf.at[slot], dbuf.at[slot], dps_sem.at[i], dpr_sem.at[i], to),
                remote(mbuf.at[slot], mbuf.at[slot], mps_sem.at[i], mpr_sem.at[i], to))

    def send_peer(i, _):
        for copy in peer_copies(i, False):
            copy.start()
        return 0

    def forward(i, _):
        for copy in peer_copies(i, True):
            copy.wait_recv()
        for copy in partner_copies(i, False):
            copy.start()
        return 0

    def from_partner(i, _):
        for copy in partner_copies(i, True):
            copy.wait_recv()
        return 0

    lax.fori_loop(1, NZ, send_peer, 0)
    for copy in partner_copies(0, False):
        copy.start()
    noise = noise_ref[...]
    scale = 1.0 / (noise * scale_root)
    misfit = ((obs_ref[...] - own_pred) / noise + pert_ref[...]).astype(jnp.bfloat16)
    misfit_wide = misfit.astype(jnp.float32)
    squares = misfit_wide * misfit_wide
    lax.fori_loop(1, NZ, forward, 0)
    lax.fori_loop(0, NZ, from_partner, 0)

    centre = jnp.sum(mbuf[...], axis=0) * (1.0 / N_GRP)

    def scaled_of(group):
        d = dbuf[group].astype(jnp.float32)
        wide = jnp.concatenate([d[:j_dev], d[j_dev:]], axis=1)
        return (wide + (mbuf[group] - centre)) * scale

    def scale_pair(n, _):
        both = jnp.concatenate([scaled_of(2 * n), scaled_of(2 * n + 1)], axis=0)
        rows = 2 * j_dev
        sbuf[pl.ds(pl.multiple_of(n * rows, 16), rows), :] = both.astype(jnp.bfloat16)
        return 0

    lax.fori_loop(0, NZ, scale_pair, 0)
    left = jnp.concatenate([scaled_of(g), misfit_wide], axis=0).astype(jnp.bfloat16)
    sums = lax.dot_general(left, sbuf[...], (((1,), (1,)), ((), ())), preferred_element_type=jnp.float32)

    n_row, n_col = j_dev // 8, members // 128
    n_gram = n_row * n_col
    n_tiles = 2 * n_gram + 1
    for h in range(2):
        for i in range(n_row):
            for c in range(n_col):
                t = h * (n_gram + 1) + i * n_col + c
                part[t] = sums[h * j_dev + 8 * i : h * j_dev + 8 * i + 8, 128 * c : 128 * c + 128]
    folded = squares[0:8]
    for i in range(1, n_row):
        folded = folded + squares[8 * i : 8 * i + 8]
    lanes = folded[:, 0:128]
    for c in range(1, n_obs // 128):
        lanes = lanes + folded[:, 128 * c : 128 * c + 128]
    part[n_gram] = lanes

    def send_part(i, _):
        t = (v + i) % n_tiles

        @pl.when(t != v)
        def _():
            remote(part.at[t], rbuf.at[v], rs_sem, rr_sem, {"vox": t}).start()

        return 0

    lax.fori_loop(0, n_tiles, send_part, 0)

    @pl.when(v < n_tiles)
    def _():
        rbuf[v] = part[v]
        got = rbuf.at[pl.ds(0, N_VOX - 1)]
        pltpu.make_async_copy(got, got, rr_sem).wait()
        tot[v] = jnp.sum(rbuf[...], axis=0)

        def spread(i, _):
            remote(tot.at[v], tot.at[v], as_sem, ar_sem, {"vox": (v + i) % N_VOX}).start()
            return 0

        lax.fori_loop(1, N_VOX, spread, 0)
        most = tot.at[pl.ds(0, n_tiles - 1)]
        pltpu.make_async_copy(most, most, ar_sem).wait()

    @pl.when(v >= n_tiles)
    def _():
        whole = tot.at[pl.ds(0, n_tiles)]
        pltpu.make_async_copy(whole, whole, ar_sem).wait()

    gbuf[g] = tot[0 : n_gram + 1]

    def rows_copy(i, arriving):
        slot = gbuf.at[((z + NZ - i) % NZ) * NC + core if arriving else g]
        return remote(slot, slot, gs_sem.at[i], gr_sem.at[i], {"grp": z_peer(i)})

    def rows_partner(i, arriving):
        slot = gbuf.at[((z + NZ - i) % NZ) * NC + (1 - core if arriving else core)]
        return remote(slot, slot, gps_sem.at[i], gpr_sem.at[i], {"grp": partner})

    def rows_send(i, _):
        rows_copy(i, False).start()
        return 0

    def rows_forward(i, _):
        rows_copy(i, True).wait_recv()
        rows_partner(i, False).start()
        return 0

    def rows_from(i, _):
        rows_partner(i, True).wait_recv()
        return 0

    lax.fori_loop(1, NZ, rows_send, 0)
    rows_partner(0, False).start()
    for i in range(n_row):
        for c in range(n_col):
            cross_ref[8 * i : 8 * i + 8, 128 * c : 128 * c + 128] = tot[n_gram + 1 + i * n_col + c]
    lax.fori_loop(1, NZ, rows_forward, 0)
    lax.fori_loop(0, NZ, rows_from, 0)

    def place(n, _):
        for i in range(n_row):
            row = pl.multiple_of(n * j_dev + 8 * i, 8)
            for c in range(n_col):
                gram_ref[pl.ds(row, 8), 128 * c : 128 * c + 128] = gbuf[n, i * n_col + c]
        return 0

    lax.fori_loop(0, N_GRP, place, 0)
    squares_all = jnp.sum(gbuf[:, n_gram], axis=0)
    damping = jnp.sum(squares_all, keepdims=True) * (1.0 / (members * n_obs * N_VOX))
    damp_ref[...] = jnp.broadcast_to(damping, TILE)

    for i in range(1, NX):
        x_copy(i)[0].wait_send()

    def y_sent(n, _):
        step, xi = n // NX + 1, far(n % NX)
        low = n % NX < NX // 2

        @pl.when((step < last) | low)
        def _():
            y_copy(0, step, xi, False)[0].wait_send()

        @pl.when((step < last) | jnp.logical_not(low))
        def _():
            y_copy(1, step, xi, False)[0].wait_send()

        return 0

    lax.fori_loop(0, last * NX, y_sent, 0)

    def grp_sent(i, _):
        for copy in (*peer_copies(i, False), rows_copy(i, False)):
            copy.wait_send()
        return 0

    def partner_sent(i, _):
        for copy in (*partner_copies(i, False), rows_partner(i, False)):
            copy.wait_send()
        return 0

    lax.fori_loop(1, NZ, grp_sent, 0)
    lax.fori_loop(0, NZ, partner_sent, 0)

    @pl.when(v < n_tiles)
    def _():
        sent = part.at[pl.ds(0, n_tiles - 1)]
        pltpu.make_async_copy(sent, sent, rs_sem).wait()
        spread_all = rbuf.at[pl.ds(0, N_VOX - 1)]
        pltpu.make_async_copy(spread_all, spread_all, as_sem).wait()

    @pl.when(v >= n_tiles)
    def _():
        sent = part.at[pl.ds(0, n_tiles)]
        pltpu.make_async_copy(sent, sent, rs_sem).wait()


def exchange(log_modulus, basis, sensitivity, blocks, observed, noise, perturbation):
    j_dev, vox_dev = log_modulus.shape
    block_vox, width = basis.shape
    blocks_dev = vox_dev // block_vox
    n_obs = sensitivity.shape[0]
    members = j_dev * N_GRP
    n_gram = (j_dev // 8) * (members // 128)
    n_tiles = 2 * n_gram + 1
    f32, bf16 = jnp.float32, jnp.bfloat16
    dma = pltpu.SemaphoreType.DMA
    vmem = pl.BlockSpec(memory_space=pltpu.VMEM)
    return pl.pallas_call(
        exchange_kernel,
        out_shape=(
            jax.ShapeDtypeStruct((members, members), f32),
            jax.ShapeDtypeStruct((j_dev, members), f32),
            jax.ShapeDtypeStruct(TILE, f32),
        ),
        in_specs=[vmem] * 7,
        out_specs=(vmem,) * 3,
        scratch_shapes=[
            pltpu.VMEM((NY, NX, blocks_dev * j_dev, width), bf16),
            pltpu.VMEM((width, n_obs), bf16),
            pltpu.VMEM((j_dev, n_obs), f32),
            pltpu.VMEM((N_GRP, 2 * j_dev, n_obs // 2), bf16),
            pltpu.VMEM((N_GRP, 1, n_obs), f32),
            pltpu.VMEM((members, n_obs), bf16),
            pltpu.VMEM((n_tiles, *TILE), f32),
            pltpu.VMEM((N_VOX, *TILE), f32),
            pltpu.VMEM((n_tiles, *TILE), f32),
            pltpu.VMEM((N_GRP, n_gram + 1, *TILE), f32),
            dma((NX,)), dma((NX,)), dma((2, NY // 2, NX)), dma((2, NY // 2, NX)),
            dma((NZ,)), dma((NZ,)), dma((NZ,)), dma((NZ,)),
            dma((NZ,)), dma((NZ,)), dma((NZ,)), dma((NZ,)),
            dma, dma, dma, dma,
            dma((NZ,)), dma((NZ,)), dma((NZ,)), dma((NZ,)),
        ],
        compiler_params=pltpu.CompilerParams(
            collective_id=0, has_side_effects=True, vmem_limit_bytes=40 << 20
        ),
        name="exchange",
    )(log_modulus, basis, sensitivity, blocks, observed, noise, perturbation)


def product(a, b):
    return lax.dot_general(
        a, b, (((1,), (0,)), ((), ())), precision=HIGHEST, preferred_element_type=jnp.float32
    )


def inverse(d, k):
    n = d.shape[0]
    lane = lax.broadcasted_iota(jnp.int32, (1, n), 1)
    sub = lax.broadcasted_iota(jnp.int32, (n, 1), 0)
    for p in range(0, n, k):
        cols = [jnp.broadcast_to(d[:, p + j : p + j + 1], (n, n)) for j in range(k)]
        s = [[cols[j][p + i : p + i + 1] for j in range(k)] for i in range(k)]
        inside = (lane >= p) & (lane < p + k)
        rows = [
            jnp.where(inside, (lane == p + i).astype(jnp.float32), d[p + i : p + i + 1])
            for i in range(k)
        ]
        for i in range(k):
            inv = 1.0 / s[i][i]
            rows[i] = rows[i] * inv
            for j in range(i + 1, k):
                s[i][j] = s[i][j] * inv
            for r in range(k):
                if r != i:
                    rows[r] = rows[r] - s[r][i] * rows[i]
                    for j in range(i + 1, k):
                        s[r][j] = s[r][j] - s[r][i] * s[i][j]
        row_in = (sub >= p) & (sub < p + k)
        d = jnp.where(inside | row_in, 0.0, d)
        for j in range(k):
            d = d - jnp.where(row_in, jnp.where(sub == p + j, -1.0, 0.0), cols[j]) * rows[j]
    return d


def solve_kernel(gram_ref, cross_ref, damp_ref, out_ref):
    b = SIDE
    damp = damp_ref[0:1, :]
    eye = lax.broadcasted_iota(jnp.int32, (b, b), 0) == lax.broadcasted_iota(jnp.int32, (b, b), 1)

    def block(i, j):
        found = gram_ref[i * b : (i + 1) * b, j * b : (j + 1) * b]
        return found + jnp.where(eye, damp, 0.0) if i == j else found

    c0, c1, c2 = (cross_ref[:, i * b : (i + 1) * b] for i in range(3))
    a01, a02, a12 = block(0, 1), block(0, 2), block(1, 2)
    a10, a20, a21 = block(1, 0), block(2, 0), block(2, 1)
    i0 = inverse(block(0, 0), PIVOTS)
    u01 = product(i0, a01)
    u02 = product(i0, a02)
    y0 = product(c0, i0)
    i1 = inverse(block(1, 1) - product(a10, u01), PIVOTS)
    a12 = a12 - product(a10, u02)
    a21 = a21 - product(a20, u01)
    a22 = block(2, 2) - product(a20, u02)
    z1 = c1 - product(y0, a01)
    z2 = c2 - product(y0, a02)
    u12 = product(i1, a12)
    y1 = product(z1, i1)
    i2 = inverse(a22 - product(a21, u12), PIVOTS)
    z2 = z2 - product(y1, a12)
    x2 = product(z2, i2)
    x1 = product(z1 - product(x2, a21), i1)
    x0 = product(c0 - product(x1, a10) - product(x2, a20), i0)
    out_ref[...] = jnp.concatenate([x0, x1, x2], axis=1)


def solve(gram, cross, damping):
    vmem = pl.BlockSpec(memory_space=pltpu.VMEM)
    return pl.pallas_call(
        solve_kernel,
        out_shape=jax.ShapeDtypeStruct(cross.shape, jnp.float32),
        in_specs=[vmem] * 3,
        out_specs=vmem,
        compiler_params=pltpu.CompilerParams(vmem_limit_bytes=32 << 20),
        name="solve",
    )(gram, cross, damping)


def on_device(log_modulus, basis, sensitivity, obs_block, observed, noise_scale, perturbation):
    n_obs = sensitivity.shape[0]
    members = log_modulus.shape[0] * N_GRP
    anomaly = lax.all_gather(log_modulus.astype(jnp.bfloat16), "grp", axis=0, tiled=True)
    gram, cross, damping = exchange(
        log_modulus, basis, sensitivity, obs_block.reshape(1, n_obs),
        observed.reshape(1, n_obs), noise_scale.reshape(1, n_obs), perturbation,
    )
    weights = solve(gram, cross, damping).astype(jnp.bfloat16)
    mixture = jnp.dot(weights, anomaly, preferred_element_type=jnp.float32)
    return log_modulus + mixture / math.sqrt(members - 1)


def solution(mesh):
    in_specs = (
        P("grp", "vox"), P(), P("vox", None), P("vox", None), P("vox"), P("vox"), P("grp", "vox"),
    )
    return jax.shard_map(
        on_device, mesh=mesh, in_specs=in_specs, out_specs=P("grp", "vox"), check_vma=False
    )
```

profile of v0, /device:TPU:1, one launch (start us, length us, event | category | flops | bytes accessed | tf_op | source)
XLA Modules:
  0.0 120.3 jit_solution(16792531442914895599)
XLA Ops:
  6.5 0.0 all-gather.2.cloned.1.call-start
  6.5 1.9 %convert_element_type.7 = bf16[24,8192]{1,0:T(8,128)(2,1)} convert(f32[24,8192]{1,0:T(8,128)} %lm_ref.1) | non-fusion elementwise | flops 196608 | bytes 1179648 | tf_op jit(solution)/shard_map/convert_element_type | solution.py:490
  8.5 0.0 all-gather.2.cloned.1.call-update
  8.5 0.0 copy-start
  8.5 1.1 copy-done
  9.6 0.0 copy-start.1
  9.6 0.9 copy-done.1
  10.6 0.0 copy-start.2
  10.6 0.9 copy-done.2
  11.5 0.0 copy-start.3
  11.5 0.9 copy-done.3
  12.4 0.0 copy-start.4
  12.4 0.7 copy-done.4
  13.1 0.0 copy-start.5
  13.1 0.7 copy-done.5
  13.8 0.0 copy-start.6
  13.8 0.7 copy-done.6
  14.5 78.0 %exchange.1 = (f32[384,384]{1,0:T(8,128)S(1)}, f32[24,384]{1,0:T(8,128)S(1)}, f32[8,128]{1,0:T(8,128)S(1)}) custom-call(f32[24,8192]{1,0:T(8,128)S(1)} %copy-done, bf16[1024,128]{1,0:T(8,128)(2,1)S(1)} %copy-done.1, bf16[1024,128]{1,0:T(8,128)(2,1)S(1)} %copy-done.2, s32[1,1024]{1,0:T(1,128)S(1)} %bitcast.4, f32[1,1024]{1,0:T(1,128)S(1)} %bitcast.5, ...), custom_call_target="tpu_custom_call" | custom-call | tf_op jit(solution)/shard_map/exchange/pallas_call | solution.py:375
  92.5 16.2 %solve.1 = f32[24,384]{1,0:T(8,128)S(1)} custom-call(f32[384,384]{1,0:T(8,128)S(1)} %get-tuple-element.8.gram_ref, f32[24,384]{1,0:T(8,128)S(1)} %get-tuple-element.9.cross_ref, f32[8,128]{1,0:T(8,128)S(1)} %get-tuple-element.10.damp_ref), custom_call_target="tpu_custom_call" | custom-call | tf_op jit(solution)/shard_map/solve/pallas_call | solution.py:477
  108.7 0.0 all-gather.2.cloned.1.call-done
  108.7 4.8 %fusion = f32[24,8192]{1,0:T(8,128)} fusion(f32[24,8192]{1,0:T(8,128)} %lm_ref.1, bf16[384,8192]{1,0:T(8,128)(2,1)} %all-gather.2.cloned.1.call-done, f32[24,384]{1,0:T(8,128)S(1)} %solve.1), kind=kOutput, calls=%fused_computation.1 | convolution fusion | flops 151397376 | bytes 7901184 | tf_op jit(solution)/shard_map/dot_general | solution.py:496
Async XLA Ops:
  6.5 102.1 %all-gather.2.cloned.1.call-start = ((), (), s32[]{:S(2)}) async-start(), calls=%async_computation | async-start | bytes 6684672 | tf_op jit(solution)/shard_map/all_gather | solution.py:490
  8.5 1.1 copy-start
  9.6 0.9 copy-start.1
  10.6 0.9 copy-start.2
  11.5 0.9 copy-start.3
  12.4 0.7 copy-start.4
  13.1 0.7 copy-start.5
  13.8 0.7 copy-start.6
Sparse Core Ops, SparseCore 0:
  9.5 64.4 all-gather.1
where the time goes:
time: 121 us; the launch traced here: 120 us
  Pallas kernels  94.2 us (78%)
  between operations  13.4 us (11%)
  local copies, waits for them, and re-layouts  5.98 us (5%)
  matrix products  4.78 us (4%)
  other arithmetic  1.92 us (2%)
    pallas_call x1, Pallas kernels, exchange(): pl.pallas_call(exchange_kernel, out_shape=(jax.ShapeDtypeStruct((members,...  78 us
    pallas_call x1, Pallas kernels, solve(): pl.pallas_call(solve_kernel, out_shape=jax.ShapeDtypeStruct(cross.shape,...  16.2 us
    unnamed x14, local copies, waits for them, and re-layouts  5.98 us
    dot_general x1, matrix products, on_device(): mixture = jnp.dot(weights, anomaly, preferred_element_type=jnp.float32)  4.78 us
  transfers between devices with their start and end apart: 1, of which 0 were waited for; matrix products, arithmetic and copies ran while one was open for 0% of the time, Pallas kernels for 78%

commit v1 on v0

--- a/solution.py
+++ b/solution.py
@@ -24,13 +24,15 @@
     )
 
 
-def exchange_kernel(
-    lm_ref, basis_ref, sens_ref, blk_ref, obs_ref, noise_ref, pert_ref,
-    gram_ref, cross_ref, damp_ref,
+def update_kernel(
+    lm_hbm, basis_hbm, sens_hbm, blk_ref, obs_ref, noise_ref, pert_hbm,
+    out_ref,
+    lm_ref, basis_ref, sens_ref, pert_ref, in_sem, abuf, gram_ref, cross_ref,
     fbuf, sens_t, pred, dbuf, mbuf, sbuf, part, rbuf, tot, gbuf,
     xs_sem, xr_sem, ys_sem, yr_sem,
     ds_sem, dr_sem, ms_sem, mr_sem, dps_sem, dpr_sem, mps_sem, mpr_sem,
     rs_sem, rr_sem, as_sem, ar_sem, gs_sem, gr_sem, gps_sem, gpr_sem,
+    fs_sem, fr_sem, fps_sem, fpr_sem,
 ):
     g = lax.axis_index("grp")
     v = lax.axis_index("vox")
@@ -45,6 +47,14 @@
     members = j_dev * N_GRP
     scale_root = math.sqrt(members - 1)
 
+    fetches = [
+        pltpu.make_async_copy(src, dst, in_sem.at[i])
+        for i, (src, dst) in enumerate(
+            ((lm_hbm, lm_ref), (basis_hbm, basis_ref), (sens_hbm, sens_ref), (pert_hbm, pert_ref))
+        )
+    ]
+    for fetch in fetches:
+        fetch.start()
     barrier = pltpu.get_barrier_semaphore()
 
     def greet_vox(i, _):
@@ -62,6 +72,8 @@
     lax.fori_loop(1, NZ, greet_grp, 0)
     pl.semaphore_signal(barrier, inc=1, device_id={"grp": partner}, device_id_type=MESH)
 
+    fetches[0].wait()
+    fetches[1].wait()
     lm = lm_ref[...]
     compliance = jnp.exp(-lm)
     stacked = jnp.concatenate(
@@ -69,7 +81,40 @@
     ).astype(jnp.bfloat16)
     features = jnp.dot(stacked, basis_ref[...], preferred_element_type=jnp.float32)
     fbuf[y, x] = features.astype(jnp.bfloat16)
+    lane_half = vox_dev // 2
+    abuf[g] = jnp.concatenate([lm[:, :lane_half], lm[:, lane_half:]], axis=0).astype(jnp.bfloat16)
     pl.semaphore_wait(barrier, N_VOX - 1 + NZ - 1 + 1)
+
+    z_last = NZ // 2
+
+    def field_part(slot, way, step):
+        if step < z_last:
+            return abuf.at[slot]
+        return abuf.at[slot, :, pl.ds(way * (lane_half // 2), lane_half // 2)]
+
+    def field_copy(way, step, arriving):
+        turn = 1 if way == 0 else NZ - 1
+        back = step if arriving else step - 1
+        slot = ((z + (NZ - turn) * back) % NZ) * NC + core
+        ref = field_part(slot, way, step)
+        return remote(ref, ref, fs_sem.at[way, step - 1], fr_sem.at[way, step - 1],
+                      {"grp": ((z + turn) % NZ) * NC + core})
+
+    def field_partner(i, arriving):
+        slot = ((z + NZ - i) % NZ) * NC + (1 - core if arriving else core)
+        return remote(abuf.at[slot], abuf.at[slot], fps_sem.at[i], fpr_sem.at[i], {"grp": partner})
+
+    def field_step(step):
+        for way in range(2):
+            if step > 0:
+                field_copy(way, step, True).wait_recv()
+            if step < z_last:
+                field_copy(way, step + 1, False).start()
+        if step in (0, z_last):
+            field_partner(step, False).start()
+        else:
+            field_partner(step, False).start()
+            field_partner(NZ - step, False).start()
 
     def x_copy(i):
         src = (x + NX - i) % NX
@@ -95,6 +140,8 @@
         x_copy(i)[0].start()
     y_send(0, 1, 0)
     y_send(1, 1, 0)
+    field_step(0)
+    fetches[2].wait()
     sens_t[...] = sens_ref[...].T
     pred[...] = jnp.zeros_like(pred)
     blk = blk_ref[...]
@@ -145,7 +192,9 @@
         compute(down_y, xs)
         return 0
 
-    lax.fori_loop(0, (last - 1) * NX, y_turn, 0)
+    lax.fori_loop(0, 2 * NX, y_turn, 0)
+    field_step(1)
+    lax.fori_loop(2 * NX, (last - 1) * NX, y_turn, 0)
 
     def y_last(n, _):
         xi = far(n)
@@ -203,6 +252,7 @@
         copy.start()
     noise = noise_ref[...]
     scale = 1.0 / (noise * scale_root)
+    fetches[3].wait()
     misfit = ((obs_ref[...] - own_pred) / noise + pert_ref[...]).astype(jnp.bfloat16)
     misfit_wide = misfit.astype(jnp.float32)
     squares = misfit_wide * misfit_wide
@@ -252,6 +302,7 @@
         return 0
 
     lax.fori_loop(0, n_tiles, send_part, 0)
+    field_step(2)
 
     @pl.when(v < n_tiles)
     def _():
@@ -314,7 +365,34 @@
     lax.fori_loop(0, N_GRP, place, 0)
     squares_all = jnp.sum(gbuf[:, n_gram], axis=0)
     damping = jnp.sum(squares_all, keepdims=True) * (1.0 / (members * n_obs * N_VOX))
-    damp_ref[...] = jnp.broadcast_to(damping, TILE)
+    field_step(3)
+    weights = solve(gram_ref, cross_ref, damping, lambda: field_step(z_last)).astype(jnp.bfloat16)
+
+    def field_from(i, _):
+        field_partner(i, True).wait_recv()
+        return 0
+
+    lax.fori_loop(0, NZ, field_from, 0)
+    col = lax.broadcasted_iota(jnp.int32, (members, 2 * members), 1)
+    row = lax.broadcasted_iota(jnp.int32, (members, 2 * members), 0)
+    group = jnp.floor((row.astype(jnp.float32) + 0.5) * (1.0 / j_dev)).astype(jnp.int32)
+    place_of = row + group * j_dev
+    spread_weights = jnp.concatenate(
+        [
+            jnp.dot(weights, (col == place_of + j_dev * h).astype(jnp.bfloat16),
+                    preferred_element_type=jnp.float32)
+            for h in range(2)
+        ],
+        axis=0,
+    ).astype(jnp.bfloat16)
+    piece = 512
+    for n in range(lane_half // piece):
+        cut = slice(n * piece, (n + 1) * piece)
+        field = abuf[:, :, cut].reshape(2 * members, piece)
+        mixture = jnp.dot(spread_weights, field, preferred_element_type=jnp.float32) * (1.0 / scale_root)
+        for h in range(2):
+            cols = slice(h * lane_half + n * piece, h * lane_half + (n + 1) * piece)
+            out_ref[:, cols] = lm_ref[:, cols] + mixture[h * j_dev : (h + 1) * j_dev]
 
     for i in range(1, NX):
         x_copy(i)[0].wait_send()
@@ -341,12 +419,15 @@
         return 0
 
     def partner_sent(i, _):
-        for copy in (*partner_copies(i, False), rows_partner(i, False)):
+        for copy in (*partner_copies(i, False), rows_partner(i, False), field_partner(i, False)):
             copy.wait_send()
         return 0
 
     lax.fori_loop(1, NZ, grp_sent, 0)
     lax.fori_loop(0, NZ, partner_sent, 0)
+    for way in range(2):
+        for step in range(1, z_last + 1):
+            field_copy(way, step, False).wait_send()
 
     @pl.when(v < n_tiles)
     def _():
@@ -361,7 +442,7 @@
         pltpu.make_async_copy(sent, sent, rs_sem).wait()
 
 
-def exchange(log_modulus, basis, sensitivity, blocks, observed, noise, perturbation):
+def update(log_modulus, basis, sensitivity, blocks, observed, noise, perturbation):
     j_dev, vox_dev = log_modulus.shape
     block_vox, width = basis.shape
     blocks_dev = vox_dev // block_vox
@@ -372,16 +453,21 @@
     f32, bf16 = jnp.float32, jnp.bfloat16
     dma = pltpu.SemaphoreType.DMA
     vmem = pl.BlockSpec(memory_space=pltpu.VMEM)
+    hbm = pl.BlockSpec(memory_space=pltpu.HBM)
     return pl.pallas_call(
-        exchange_kernel,
-        out_shape=(
-            jax.ShapeDtypeStruct((members, members), f32),
-            jax.ShapeDtypeStruct((j_dev, members), f32),
-            jax.ShapeDtypeStruct(TILE, f32),
-        ),
-        in_specs=[vmem] * 7,
-        out_specs=(vmem,) * 3,
+        update_kernel,
+        out_shape=jax.ShapeDtypeStruct((j_dev, vox_dev), f32),
+        in_specs=[hbm, hbm, hbm, vmem, vmem, vmem, hbm],
+        out_specs=vmem,
         scratch_shapes=[
+            pltpu.VMEM((j_dev, vox_dev), f32),
+            pltpu.VMEM((block_vox, width), bf16),
+            pltpu.VMEM((n_obs, width), bf16),
+            pltpu.VMEM((j_dev, n_obs), f32),
+            dma((4,)),
+            pltpu.VMEM((N_GRP, 2 * j_dev, vox_dev // 2), bf16),
+            pltpu.VMEM((members, members), f32),
+            pltpu.VMEM((j_dev, members), f32),
             pltpu.VMEM((NY, NX, blocks_dev * j_dev, width), bf16),
             pltpu.VMEM((width, n_obs), bf16),
             pltpu.VMEM((j_dev, n_obs), f32),
@@ -397,11 +483,12 @@
             dma((NZ,)), dma((NZ,)), dma((NZ,)), dma((NZ,)),
             dma, dma, dma, dma,
             dma((NZ,)), dma((NZ,)), dma((NZ,)), dma((NZ,)),
+            dma((2, NZ // 2)), dma((2, NZ // 2)), dma((NZ,)), dma((NZ,)),
         ],
         compiler_params=pltpu.CompilerParams(
-            collective_id=0, has_side_effects=True, vmem_limit_bytes=40 << 20
+            collective_id=0, has_side_effects=True, vmem_limit_bytes=62 << 20
         ),
-        name="exchange",
+        name="update",
     )(log_modulus, basis, sensitivity, blocks, observed, noise, perturbation)
 
 
@@ -440,9 +527,8 @@
     return d
 
 
-def solve_kernel(gram_ref, cross_ref, damp_ref, out_ref):
+def solve(gram_ref, cross_ref, damp, between):
     b = SIDE
-    damp = damp_ref[0:1, :]
     eye = lax.broadcasted_iota(jnp.int32, (b, b), 0) == lax.broadcasted_iota(jnp.int32, (b, b), 1)
 
     def block(i, j):
@@ -462,6 +548,7 @@
     a22 = block(2, 2) - product(a20, u02)
     z1 = c1 - product(y0, a01)
     z2 = c2 - product(y0, a02)
+    between()
     u12 = product(i1, a12)
     y1 = product(z1, i1)
     i2 = inverse(a22 - product(a21, u12), PIVOTS)
@@ -469,32 +556,15 @@
     x2 = product(z2, i2)
     x1 = product(z1 - product(x2, a21), i1)
     x0 = product(c0 - product(x1, a10) - product(x2, a20), i0)
-    out_ref[...] = jnp.concatenate([x0, x1, x2], axis=1)
-
-
-def solve(gram, cross, damping):
-    vmem = pl.BlockSpec(memory_space=pltpu.VMEM)
-    return pl.pallas_call(
-        solve_kernel,
-        out_shape=jax.ShapeDtypeStruct(cross.shape, jnp.float32),
-        in_specs=[vmem] * 3,
-        out_specs=vmem,
-        compiler_params=pltpu.CompilerParams(vmem_limit_bytes=32 << 20),
-        name="solve",
-    )(gram, cross, damping)
+    return jnp.concatenate([x0, x1, x2], axis=1)
 
 
 def on_device(log_modulus, basis, sensitivity, obs_block, observed, noise_scale, perturbation):
     n_obs = sensitivity.shape[0]
-    members = log_modulus.shape[0] * N_GRP
-    anomaly = lax.all_gather(log_modulus.astype(jnp.bfloat16), "grp", axis=0, tiled=True)
-    gram, cross, damping = exchange(
+    return update(
         log_modulus, basis, sensitivity, obs_block.reshape(1, n_obs),
         observed.reshape(1, n_obs), noise_scale.reshape(1, n_obs), perturbation,
     )
-    weights = solve(gram, cross, damping).astype(jnp.bfloat16)
-    mixture = jnp.dot(weights, anomaly, preferred_element_type=jnp.float32)
-    return log_modulus + mixture / math.sqrt(members - 1)
 
 
 def solution(mesh):

time: 121 us -> 96.6 us (0.80)
  between operations: 13.4 us -> 0.01 us
  matrix products: 4.78 us -> 0 us
  local copies, waits for them, and re-layouts: 5.98 us -> 2.06 us
  other arithmetic: 1.92 us -> 0 us
    dot_general x1 -> x0, matrix products: 4.78 us -> none  [on_device(): mixture = jnp.dot(weights, anomaly, preferred_element_type=jnp.float32)]
    unnamed x14 -> x1, local copies, waits for them, and re-layouts: 5.98 us -> 2.06 us
    convert_element_type x1 -> x0, other arithmetic: 1.92 us -> none  [on_device(): log_modulus.astype(jnp.bfloat16)]
    pallas_call x2 -> x1, Pallas kernels: 94.2 us -> 94.3 us  [update(): pl.pallas_call(update_kernel, out_shape=jax.ShapeDtypeStruct((j_dev, vox_...]
  transfers between devices with their start and end apart: 1 -> 0, of which waited for: 0 -> 0; matrix products, arithmetic and copies ran while one was open for 0% -> 0% of each run, Pallas kernels for 78% -> 0%
where the time goes in v1:
time: 96.6 us; the launch traced here: 96.3 us
  Pallas kernels  94.3 us (98%)
  local copies, waits for them, and re-layouts  2.06 us (2%)
    pallas_call x1, Pallas kernels, update(): pl.pallas_call(update_kernel, out_shape=jax.ShapeDtypeStruct((j_dev, vox_...  94.3 us
    unnamed x1, local copies, waits for them, and re-layouts  2.06 us

profile of v1, /device:TPU:1, one launch (start us, length us, event | category | flops | bytes accessed | tf_op | source)
XLA Modules:
  0.0 96.3 jit_solution(4612197923773947055)
XLA Ops:
  0.0 94.3 %update.1 = f32[24,8192]{1,0:T(8,128)} custom-call(f32[24,8192]{1,0:T(8,128)} %lm_hbm.1, bf16[1024,128]{1,0:T(8,128)(2,1)} %basis_hbm.1, bf16[1024,128]{1,0:T(8,128)(2,1)} %sens_hbm.1, s32[1,1024]{1,0:T(1,128)} %bitcast.3, f32[1,1024]{1,0:T(1,128)} %bitcast.4, f32[1,1024]{1,0:T(1,128)} %bitcast.5, f32[24,1024]{1,0:T(8,128)} %pert_hbm.1), custom_call_target="tpu_custom_call" | custom-call | tf_op jit(solution)/shard_map/update/pallas_call | solution.py:457
  94.3 2.1 %copy.9 = f32[24,8192]{1,0:T(8,128)} copy(f32[24,8192]{1,0:T(8,128)} %update.1) | data formatting | bytes 1572864

commit v2 on v1

--- a/solution.py
+++ b/solution.py
@@ -15,6 +15,8 @@
 SIDE = 128
 PIVOTS = 4
 TILE = (8, 128)
+CAP = 8
+ROWS = 16
 
 
 def remote(src, dst, send_sem, recv_sem, device):
@@ -28,9 +30,8 @@
     lm_hbm, basis_hbm, sens_hbm, blk_ref, obs_ref, noise_ref, pert_hbm,
     out_ref,
     lm_ref, basis_ref, sens_ref, pert_ref, in_sem, abuf, gram_ref, cross_ref,
-    fbuf, sens_t, pred, dbuf, mbuf, sbuf, part, rbuf, tot, gbuf,
-    xs_sem, xr_sem, ys_sem, yr_sem,
-    ds_sem, dr_sem, ms_sem, mr_sem, dps_sem, dpr_sem, mps_sem, mpr_sem,
+    xout, xin, pbuf, phi, pred_ref, part, rbuf, tot, gbuf,
+    xs_sem, xr_sem, ds_sem, dr_sem, dps_sem, dpr_sem,
     rs_sem, rr_sem, as_sem, ar_sem, gs_sem, gr_sem, gps_sem, gpr_sem,
     fs_sem, fr_sem, fps_sem, fpr_sem,
 ):
@@ -43,16 +44,13 @@
     block_vox, width = basis_ref.shape
     blocks_dev = vox_dev // block_vox
     n_obs = sens_ref.shape[0]
-    half = n_obs // 2
     members = j_dev * N_GRP
     scale_root = math.sqrt(members - 1)
 
-    fetches = [
-        pltpu.make_async_copy(src, dst, in_sem.at[i])
-        for i, (src, dst) in enumerate(
-            ((lm_hbm, lm_ref), (basis_hbm, basis_ref), (sens_hbm, sens_ref), (pert_hbm, pert_ref))
-        )
-    ]
+    in_blocks = [slice(b * block_vox, (b + 1) * block_vox) for b in range(blocks_dev)]
+    pairs = [(lm_hbm.at[:, cut], lm_ref.at[:, cut]) for cut in in_blocks]
+    pairs += [(basis_hbm, basis_ref), (sens_hbm, sens_ref), (pert_hbm, pert_ref)]
+    fetches = [pltpu.make_async_copy(src, dst, in_sem.at[i]) for i, (src, dst) in enumerate(pairs)]
     for fetch in fetches:
         fetch.start()
     barrier = pltpu.get_barrier_semaphore()
@@ -72,18 +70,42 @@
     lax.fori_loop(1, NZ, greet_grp, 0)
     pl.semaphore_signal(barrier, inc=1, device_id={"grp": partner}, device_id_type=MESH)
 
-    fetches[0].wait()
-    fetches[1].wait()
-    lm = lm_ref[...]
-    compliance = jnp.exp(-lm)
-    stacked = jnp.concatenate(
-        [compliance[:, b * block_vox : (b + 1) * block_vox] for b in range(blocks_dev)], axis=0
-    ).astype(jnp.bfloat16)
+    strips = []
+    for b in range(blocks_dev):
+        fetches[b].wait()
+        strips.append(jnp.exp(-lm_ref[:, in_blocks[b]]))
+    stacked = jnp.concatenate(strips, axis=0).astype(jnp.bfloat16)
+    fetches[blocks_dev].wait()
     features = jnp.dot(stacked, basis_ref[...], preferred_element_type=jnp.float32)
-    fbuf[y, x] = features.astype(jnp.bfloat16)
+    wide = jnp.concatenate([features[b * j_dev : (b + 1) * j_dev] for b in range(blocks_dev)], axis=1)
+    f_half = blocks_dev * width // 2
+    pbuf[g] = jnp.concatenate([wide[:, :f_half], wide[:, f_half:]], axis=0).astype(jnp.bfloat16)
     lane_half = vox_dev // 2
-    abuf[g] = jnp.concatenate([lm[:, :lane_half], lm[:, lane_half:]], axis=0).astype(jnp.bfloat16)
     pl.semaphore_wait(barrier, N_VOX - 1 + NZ - 1 + 1)
+
+    def peer_copy(i, arriving):
+        slot = pbuf.at[((z + NZ - i) % NZ) * NC + core if arriving else g]
+        return remote(slot, slot, ds_sem.at[i], dr_sem.at[i], {"grp": z_peer(i)})
+
+    def partner_copy(i, arriving):
+        slot = pbuf.at[((z + NZ - i) % NZ) * NC + (1 - core if arriving else core)]
+        return remote(slot, slot, dps_sem.at[i], dpr_sem.at[i], {"grp": partner})
+
+    def send_peer(i, _):
+        peer_copy(i, False).start()
+        return 0
+
+    def forward(i, _):
+        peer_copy(i, True).wait_recv()
+        partner_copy(i, False).start()
+        return 0
+
+    def from_partner(i, _):
+        partner_copy(i, True).wait_recv()
+        return 0
+
+    lax.fori_loop(1, NZ, send_peer, 0)
+    partner_copy(0, False).start()
 
     z_last = NZ // 2
 
@@ -116,165 +138,106 @@
             field_partner(step, False).start()
             field_partner(NZ - step, False).start()
 
-    def x_copy(i):
-        src = (x + NX - i) % NX
-        mine = remote(fbuf.at[y, x], fbuf.at[y, x], xs_sem.at[i], xr_sem.at[i],
-                      {"vox": ((x + i) % NX) * NY + y})
-        theirs = remote(fbuf.at[y, src], fbuf.at[y, src], xs_sem.at[i], xr_sem.at[i],
-                        {"vox": ((x + i) % NX) * NY + y})
-        return mine, theirs
-
-    def y_copy(way, step, xi, arriving):
-        turn = 1 if way == 0 else NY - 1
-        xs = (x + xi) % NX
-        back = step if arriving else step - 1
-        ys = (y + (NY - turn) * back) % NY
-        slot = fbuf.at[ys, xs]
-        return remote(slot, slot, ys_sem.at[way, step - 1, xi], yr_sem.at[way, step - 1, xi],
-                      {"vox": x * NY + (y + turn) % NY}), ys, xs
-
-    def y_send(way, step, xi):
-        y_copy(way, step, xi, False)[0].start()
-
-    for i in (1, NX - 1, 2):
-        x_copy(i)[0].start()
-    y_send(0, 1, 0)
-    y_send(1, 1, 0)
+    n_blocks = blocks_dev * N_VOX
+    slots = blocks_dev * CAP
+    groups = slots // ROWS
+    blk = blk_ref[...]
+    hit = (lax.broadcasted_iota(jnp.int32, (n_blocks, n_obs), 0) == blk).astype(jnp.float32)
+    before = (
+        lax.broadcasted_iota(jnp.int32, (n_obs, n_obs), 0)
+        < lax.broadcasted_iota(jnp.int32, (n_obs, n_obs), 1)
+    ).astype(jnp.float32)
+    counts = jnp.dot(
+        hit.astype(jnp.bfloat16), before.astype(jnp.bfloat16), preferred_element_type=jnp.float32
+    )
+    rank = jnp.sum(hit * counts, axis=0, keepdims=True)
+    slot_of = blk * CAP + rank.astype(jnp.int32)
+
+    def three(value):
+        first = value.astype(jnp.bfloat16).astype(jnp.float32)
+        second = (value - first).astype(jnp.bfloat16).astype(jnp.float32)
+        return first, second, value - first - second
+
+    observed = obs_ref[...]
+    sub = lax.broadcasted_iota(jnp.int32, (8, n_obs), 0)
+    tail = jnp.zeros((8, n_obs), jnp.float32)
+    for i, term in enumerate((*three(observed), *three(1.0 / noise_ref[...]))):
+        tail = jnp.where(sub == i, term, tail)
+    fetches[blocks_dev + 1].wait()
+    fetches[blocks_dev + 2].wait()
+    with_obs = jnp.concatenate([pert_ref[...], tail], axis=0).astype(jnp.bfloat16)
+    row_id = lax.broadcasted_iota(jnp.int32, (N_VOX * ROWS, n_obs), 0)
+    code = row_id + (slots - ROWS) * lax.shift_right_logical(row_id, ROWS.bit_length() - 1)
+    extras = []
+    for q in range(groups):
+        take = (code == slot_of - ROWS * q).astype(jnp.float32).astype(jnp.bfloat16)
+        rows_q = jnp.dot(take, sens_ref[...], preferred_element_type=jnp.float32)
+        xout[:, ROWS * q : ROWS * (q + 1), :] = rows_q.astype(jnp.bfloat16).reshape(N_VOX, ROWS, width)
+        extras.append(
+            lax.dot_general(take, with_obs, (((1,), (1,)), ((), ())), preferred_element_type=jnp.float32)
+        )
+    beside = jnp.concatenate(extras, axis=1).astype(jnp.bfloat16)
+    xout[:, slots : slots + ROWS, :] = beside.reshape(N_VOX, ROWS, width)
+
+    def send_rows(i, _):
+        to = (v + i) % N_VOX
+        remote(xout.at[to], xin.at[v], xs_sem, xr_sem, {"vox": to}).start()
+        return 0
+
+    lax.fori_loop(1, N_VOX, send_rows, 0)
+    xin[v] = xout[v]
+    lm = lm_ref[...]
+    abuf[g] = jnp.concatenate([lm[:, :lane_half], lm[:, lane_half:]], axis=0).astype(jnp.bfloat16)
     field_step(0)
-    fetches[2].wait()
-    sens_t[...] = sens_ref[...].T
-    pred[...] = jnp.zeros_like(pred)
-    blk = blk_ref[...]
-
-    def compute(ys, xs):
-        all_pred = jnp.dot(fbuf[ys, xs], sens_t[...], preferred_element_type=jnp.float32)
-        first = (xs * NY + ys) * blocks_dev
-        acc = pred[...]
-        for b in range(blocks_dev):
-            acc = jnp.where(blk == first + b, all_pred[b * j_dev : (b + 1) * j_dev], acc)
-        pred[...] = acc
-
-    compute(y, x)
-
-    def far(n):
-        return n + n // 2 - 2 * (n // 3)
-
-    def x_turn(n, _):
-        xi = far(n)
-        i = NX - xi
-        x_copy(i)[1].wait_recv()
-        y_send(0, 1, xi)
-        y_send(1, 1, xi)
-        compute(y, (x + xi) % NX)
-        return 0
-
-    lax.fori_loop(1, NX, x_turn, 0)
-    last = NY // 2
-
-    def y_turn(n, _):
-        step, xi = n // NX + 1, far(n % NX)
-        low = n % NX < NX // 2
-        up, up_y, xs = y_copy(0, step, xi, True)
-        up.wait_recv()
-
-        @pl.when((step + 1 < last) | low)
-        def _():
-            y_send(0, step + 1, xi)
-
-        down, down_y, _ = y_copy(1, step, xi, True)
-        down.wait_recv()
-
-        @pl.when((step + 1 < last) | jnp.logical_not(low))
-        def _():
-            y_send(1, step + 1, xi)
-
-        compute(up_y, xs)
-        compute(down_y, xs)
-        return 0
-
-    lax.fori_loop(0, 2 * NX, y_turn, 0)
-    field_step(1)
-    lax.fori_loop(2 * NX, (last - 1) * NX, y_turn, 0)
-
-    def y_last(n, _):
-        xi = far(n)
-
-        @pl.when(n < NX // 2)
-        def _():
-            y_copy(0, last, xi, True)[0].wait_recv()
-
-        @pl.when(n >= NX // 2)
-        def _():
-            y_copy(1, last, xi, True)[0].wait_recv()
-
-        compute((y + last) % NY, (x + xi) % NX)
-        return 0
-
-    lax.fori_loop(0, NX, y_last, 0)
-
-    own_pred = pred[...]
-    own_mean = jnp.mean(own_pred, axis=0, keepdims=True)
-    mbuf[g] = own_mean
-    dev = own_pred - own_mean
-    dbuf[g] = jnp.concatenate([dev[:, :half], dev[:, half:]], axis=0).astype(jnp.bfloat16)
-
-    def peer_copies(i, arriving):
-        slot = ((z + NZ - i) % NZ) * NC + core if arriving else g
-        to = {"grp": z_peer(i)}
-        return (remote(dbuf.at[slot], dbuf.at[slot], ds_sem.at[i], dr_sem.at[i], to),
-                remote(mbuf.at[slot], mbuf.at[slot], ms_sem.at[i], mr_sem.at[i], to))
-
-    def partner_copies(i, arriving):
-        slot = ((z + NZ - i) % NZ) * NC + (1 - core if arriving else core)
-        to = {"grp": partner}
-        return (remote(dbuf.at[slot], dbuf.at[slot], dps_sem.at[i], dpr_sem.at[i], to),
-                remote(mbuf.at[slot], mbuf.at[slot], mps_sem.at[i], mpr_sem.at[i], to))
-
-    def send_peer(i, _):
-        for copy in peer_copies(i, False):
-            copy.start()
-        return 0
-
-    def forward(i, _):
-        for copy in peer_copies(i, True):
-            copy.wait_recv()
-        for copy in partner_copies(i, False):
-            copy.start()
-        return 0
-
-    def from_partner(i, _):
-        for copy in partner_copies(i, True):
-            copy.wait_recv()
-        return 0
-
-    lax.fori_loop(1, NZ, send_peer, 0)
-    for copy in partner_copies(0, False):
-        copy.start()
-    noise = noise_ref[...]
-    scale = 1.0 / (noise * scale_root)
-    fetches[3].wait()
-    misfit = ((obs_ref[...] - own_pred) / noise + pert_ref[...]).astype(jnp.bfloat16)
-    misfit_wide = misfit.astype(jnp.float32)
-    squares = misfit_wide * misfit_wide
     lax.fori_loop(1, NZ, forward, 0)
     lax.fori_loop(0, NZ, from_partner, 0)
 
-    centre = jnp.sum(mbuf[...], axis=0) * (1.0 / N_GRP)
-
-    def scaled_of(group):
-        d = dbuf[group].astype(jnp.float32)
-        wide = jnp.concatenate([d[:j_dev], d[j_dev:]], axis=1)
-        return (wide + (mbuf[group] - centre)) * scale
-
-    def scale_pair(n, _):
-        both = jnp.concatenate([scaled_of(2 * n), scaled_of(2 * n + 1)], axis=0)
+    def features_of(group):
+        d = pbuf[group].astype(jnp.float32)
+        return jnp.concatenate([d[:j_dev], d[j_dev:]], axis=1)
+
+    def place_pair(n, _):
+        both = jnp.concatenate([features_of(2 * n), features_of(2 * n + 1)], axis=0)
         rows = 2 * j_dev
-        sbuf[pl.ds(pl.multiple_of(n * rows, 16), rows), :] = both.astype(jnp.bfloat16)
-        return 0
-
-    lax.fori_loop(0, NZ, scale_pair, 0)
-    left = jnp.concatenate([scaled_of(g), misfit_wide], axis=0).astype(jnp.bfloat16)
-    sums = lax.dot_general(left, sbuf[...], (((1,), (1,)), ((), ())), preferred_element_type=jnp.float32)
+        phi[pl.ds(pl.multiple_of(n * rows, 16), rows), :] = both.astype(jnp.bfloat16)
+        return 0
+
+    lax.fori_loop(0, NZ, place_pair, 0)
+    field_step(1)
+    got_rows = xin.at[pl.ds(0, N_VOX - 1)]
+    pltpu.make_async_copy(got_rows, got_rows, xr_sem).wait()
+
+    n_here = N_VOX * ROWS
+    extra = xin[:, slots : slots + ROWS, :].astype(jnp.float32).reshape(n_here, width).T
+    per = width // groups
+    low = (lax.broadcasted_iota(jnp.int32, (n_here, width), 0) & (ROWS - 1)) < CAP
+    sums = jnp.zeros((2 * j_dev, members), jnp.float32)
+    lanes = jnp.zeros(TILE, jnp.float32)
+    pair = 2 * width
+    contract = (((1,), (1,)), ((), ()))
+    for q in range(groups):
+        rows_q = xin[:, ROWS * q : ROWS * (q + 1), :].astype(jnp.float32).reshape(n_here, width)
+        both = jnp.concatenate([jnp.where(low, rows_q, 0.0), jnp.where(low, 0.0, rows_q)], axis=1)
+        pred = lax.dot_general(
+            phi[:, pair * q : pair * (q + 1)], both.astype(jnp.bfloat16), contract,
+            preferred_element_type=jnp.float32,
+        )
+        pred_ref[...] = pred
+        centre = jnp.sum(pred, axis=0, keepdims=True) * (1.0 / members)
+        at = per * q + j_dev
+        seen = extra[at : at + 1] + extra[at + 1 : at + 2] + extra[at + 2 : at + 3]
+        inv_noise = extra[at + 3 : at + 4] + extra[at + 4 : at + 5] + extra[at + 5 : at + 6]
+        scale = inv_noise * (1.0 / scale_root)
+        scaled = ((pred - centre) * scale).astype(jnp.bfloat16)
+        own_pred = pred_ref[pl.ds(pl.multiple_of(g * j_dev, 8), j_dev), :]
+        misfit = (seen - own_pred) * inv_noise + extra[per * q : per * q + j_dev]
+        misfit = misfit.astype(jnp.bfloat16).astype(jnp.float32)
+        left = jnp.concatenate([(own_pred - centre) * scale, misfit], axis=0).astype(jnp.bfloat16)
+        sums = sums + lax.dot_general(left, scaled, contract, preferred_element_type=jnp.float32)
+        squares = misfit * misfit
+        for i in range(j_dev // 8):
+            for c in range(n_here // 128):
+                lanes = lanes + squares[8 * i : 8 * i + 8, 128 * c : 128 * c + 128]
 
     n_row, n_col = j_dev // 8, members // 128
     n_gram = n_row * n_col
@@ -284,12 +247,6 @@
             for c in range(n_col):
                 t = h * (n_gram + 1) + i * n_col + c
                 part[t] = sums[h * j_dev + 8 * i : h * j_dev + 8 * i + 8, 128 * c : 128 * c + 128]
-    folded = squares[0:8]
-    for i in range(1, n_row):
-        folded = folded + squares[8 * i : 8 * i + 8]
-    lanes = folded[:, 0:128]
-    for c in range(1, n_obs // 128):
-        lanes = lanes + folded[:, 128 * c : 128 * c + 128]
     part[n_gram] = lanes
 
     def send_part(i, _):
@@ -392,34 +349,18 @@
         mixture = jnp.dot(spread_weights, field, preferred_element_type=jnp.float32) * (1.0 / scale_root)
         for h in range(2):
             cols = slice(h * lane_half + n * piece, h * lane_half + (n + 1) * piece)
-            out_ref[:, cols] = lm_ref[:, cols] + mixture[h * j_dev : (h + 1) * j_dev]
-
-    for i in range(1, NX):
-        x_copy(i)[0].wait_send()
-
-    def y_sent(n, _):
-        step, xi = n // NX + 1, far(n % NX)
-        low = n % NX < NX // 2
-
-        @pl.when((step < last) | low)
-        def _():
-            y_copy(0, step, xi, False)[0].wait_send()
-
-        @pl.when((step < last) | jnp.logical_not(low))
-        def _():
-            y_copy(1, step, xi, False)[0].wait_send()
-
-        return 0
-
-    lax.fori_loop(0, last * NX, y_sent, 0)
+            out_ref[:, cols] = mixture[h * j_dev : (h + 1) * j_dev]
+
+    sent_rows = xout.at[pl.ds(0, N_VOX - 1)]
+    pltpu.make_async_copy(sent_rows, sent_rows, xs_sem).wait()
 
     def grp_sent(i, _):
-        for copy in (*peer_copies(i, False), rows_copy(i, False)):
-            copy.wait_send()
+        peer_copy(i, False).wait_send()
+        rows_copy(i, False).wait_send()
         return 0
 
     def partner_sent(i, _):
-        for copy in (*partner_copies(i, False), rows_partner(i, False), field_partner(i, False)):
+        for copy in (partner_copy(i, False), rows_partner(i, False), field_partner(i, False)):
             copy.wait_send()
         return 0
 
@@ -464,23 +405,20 @@
             pltpu.VMEM((block_vox, width), bf16),
             pltpu.VMEM((n_obs, width), bf16),
             pltpu.VMEM((j_dev, n_obs), f32),
-            dma((4,)),
+            dma((blocks_dev + 3,)),
             pltpu.VMEM((N_GRP, 2 * j_dev, vox_dev // 2), bf16),
             pltpu.VMEM((members, members), f32),
             pltpu.VMEM((j_dev, members), f32),
-            pltpu.VMEM((NY, NX, blocks_dev * j_dev, width), bf16),
-            pltpu.VMEM((width, n_obs), bf16),
-            pltpu.VMEM((j_dev, n_obs), f32),
-            pltpu.VMEM((N_GRP, 2 * j_dev, n_obs // 2), bf16),
-            pltpu.VMEM((N_GRP, 1, n_obs), f32),
-            pltpu.VMEM((members, n_obs), bf16),
+            pltpu.VMEM((N_VOX, blocks_dev * CAP + ROWS, width), bf16),
+            pltpu.VMEM((N_VOX, blocks_dev * CAP + ROWS, width), bf16),
+            pltpu.VMEM((N_GRP, 2 * j_dev, blocks_dev * width // 2), bf16),
+            pltpu.VMEM((members, blocks_dev * width), bf16),
+            pltpu.VMEM((members, N_VOX * ROWS), f32),
             pltpu.VMEM((n_tiles, *TILE), f32),
             pltpu.VMEM((N_VOX, *TILE), f32),
             pltpu.VMEM((n_tiles, *TILE), f32),
             pltpu.VMEM((N_GRP, n_gram + 1, *TILE), f32),
-            dma((NX,)), dma((NX,)), dma((2, NY // 2, NX)), dma((2, NY // 2, NX)),
-            dma((NZ,)), dma((NZ,)), dma((NZ,)), dma((NZ,)),
-            dma((NZ,)), dma((NZ,)), dma((NZ,)), dma((NZ,)),
+            dma, dma, dma((NZ,)), dma((NZ,)), dma((NZ,)), dma((NZ,)),
             dma, dma, dma, dma,
             dma((NZ,)), dma((NZ,)), dma((NZ,)), dma((NZ,)),
             dma((2, NZ // 2)), dma((2, NZ // 2)), dma((NZ,)), dma((NZ,)),
@@ -561,7 +499,7 @@
 
 def on_device(log_modulus, basis, sensitivity, obs_block, observed, noise_scale, perturbation):
     n_obs = sensitivity.shape[0]
-    return update(
+    return log_modulus + update(
         log_modulus, basis, sensitivity, obs_block.reshape(1, n_obs),
         observed.reshape(1, n_obs), noise_scale.reshape(1, n_obs), perturbation,
     )

time: 96.6 us -> 86.5 us (0.90)
  Pallas kernels: 94.3 us -> 84.2 us
  other arithmetic: 0 us -> 2.09 us
  local copies, waits for them, and re-layouts: 2.06 us -> 0.01 us
    pallas_call x1, Pallas kernels: 94.3 us -> 84.2 us  [update(): pl.pallas_call(update_kernel, out_shape=jax.ShapeDtypeStruct((j_dev, vox_...]
    add x0 -> x1, other arithmetic: none -> 2.09 us  [on_device(): log_modulus + update(log_modulus, basis, sensitivity, obs_block.reshape(1...]
    unnamed x1 -> x2, local copies, waits for them, and re-layouts: 2.06 us -> 0.01 us
where the time goes in v2:
time: 86.5 us; the launch traced here: 86.3 us
  Pallas kernels  84.2 us (97%)
  other arithmetic  2.09 us (2%)
    pallas_call x1, Pallas kernels, update(): pl.pallas_call(update_kernel, out_shape=jax.ShapeDtypeStruct((j_dev, vox_...  84.2 us
    add x1, other arithmetic, on_device(): log_modulus + update(log_modulus, basis, sensitivity, obs_block.reshape(1...  2.09 us

profile of v2, /device:TPU:1, one launch (start us, length us, event | category | flops | bytes accessed | tf_op | source)
XLA Modules:
  0.0 86.3 jit_solution(12036597395314916147)
XLA Ops:
  0.0 0.0 copy-start
  0.0 84.2 %update.1 = f32[24,8192]{1,0:T(8,128)} custom-call(f32[24,8192]{1,0:T(8,128)} %lm_hbm.1, bf16[1024,128]{1,0:T(8,128)(2,1)} %basis_hbm.1, bf16[1024,128]{1,0:T(8,128)(2,1)} %sens_hbm.1, s32[1,1024]{1,0:T(1,128)} %bitcast.3, f32[1,1024]{1,0:T(1,128)} %bitcast.4, f32[1,1024]{1,0:T(1,128)} %bitcast.5, f32[24,1024]{1,0:T(8,128)} %pert_hbm.1), custom_call_target="tpu_custom_call" | custom-call | tf_op jit(solution)/shard_map/update/pallas_call | solution.py:398
  84.2 0.0 copy-done
  84.2 2.1 %add.3 = f32[24,8192]{1,0:T(8,128)} add(f32[24,8192]{1,0:T(8,128)S(1)} %copy-done, f32[24,8192]{1,0:T(8,128)} %update.1) | non-fusion elementwise | flops 196608 | bytes 2359296 | tf_op jit(solution)/shard_map/add | solution.py:502
Async XLA Ops:
  0.0 84.2 %copy-start = (f32[24,8192]{1,0:T(8,128)S(1)}, f32[24,8192]{1,0:T(8,128)}, u32[]{:S(2)}) copy-start(f32[24,8192]{1,0:T(8,128)} %lm_hbm.1) | copy-start | bytes 2359300

commit v3 on v2

--- a/solution.py
+++ b/solution.py
@@ -13,8 +13,10 @@
 NX, NY, NZ, NC = 4, 8, 8, 2
 N_VOX, N_GRP = NX * NY, NZ * NC
 SIDE = 128
-PIVOTS = 4
+PIVOTS = 8
 TILE = (8, 128)
+PIECE = (16, 128)
+QUAD = 4
 CAP = 8
 ROWS = 16
 
@@ -30,9 +32,9 @@
     lm_hbm, basis_hbm, sens_hbm, blk_ref, obs_ref, noise_ref, pert_hbm,
     out_ref,
     lm_ref, basis_ref, sens_ref, pert_ref, in_sem, abuf, gram_ref, cross_ref,
-    xout, xin, pbuf, phi, pred_ref, part, rbuf, tot, gbuf,
-    xs_sem, xr_sem, ds_sem, dr_sem, dps_sem, dpr_sem,
-    rs_sem, rr_sem, as_sem, ar_sem, gs_sem, gr_sem, gps_sem, gpr_sem,
+    xout, xin, pbuf, phi, pred_ref, part, rbuf, tot, gbuf, mbuf, msum,
+    xs_sem, xr_sem, hs_sem, hr_sem, cs_sem, cr_sem, ds_sem, dr_sem, dps_sem, dpr_sem,
+    rs_sem, rr_sem, as_sem, ar_sem, gs_sem, gr_sem, ms_sem, mr_sem, mps_sem, mpr_sem,
     fs_sem, fr_sem, fps_sem, fpr_sem,
 ):
     g = lax.axis_index("grp")
@@ -179,16 +181,35 @@
     beside = jnp.concatenate(extras, axis=1).astype(jnp.bfloat16)
     xout[:, slots : slots + ROWS, :] = beside.reshape(N_VOX, ROWS, width)
 
+    part_rows = slots // NC
+    own_half = pl.ds(pl.multiple_of(core * part_rows, 16), part_rows)
+    other_half = pl.ds(pl.multiple_of((1 - core) * part_rows, 16), part_rows)
+    beside_rows = pl.ds(slots, ROWS)
+
+    def half_copy(i):
+        to = (v + i) % N_VOX
+        return remote(xout.at[to, own_half], xin.at[v, own_half], hs_sem, hr_sem.at[i], {"vox": to})
+
+    def half_from(i, which):
+        slot = xin.at[(v + N_VOX - i) % N_VOX, which]
+        return remote(slot, slot, cs_sem, cr_sem, {"grp": partner})
+
     def send_rows(i, _):
         to = (v + i) % N_VOX
-        remote(xout.at[to], xin.at[v], xs_sem, xr_sem, {"vox": to}).start()
+        half_copy(i).start()
+        remote(xout.at[to, beside_rows], xin.at[v, beside_rows], xs_sem, xr_sem, {"vox": to}).start()
+        return 0
+
+    def pass_half(i, _):
+        slot = xin.at[(v + N_VOX - i) % N_VOX, own_half]
+        remote(slot, slot, hs_sem, hr_sem.at[i], {"grp": partner}).wait_recv()
+        half_from(i, own_half).start()
         return 0
 
     lax.fori_loop(1, N_VOX, send_rows, 0)
     xin[v] = xout[v]
     lm = lm_ref[...]
     abuf[g] = jnp.concatenate([lm[:, :lane_half], lm[:, lane_half:]], axis=0).astype(jnp.bfloat16)
-    field_step(0)
     lax.fori_loop(1, NZ, forward, 0)
     lax.fori_loop(0, NZ, from_partner, 0)
 
@@ -203,15 +224,21 @@
         return 0
 
     lax.fori_loop(0, NZ, place_pair, 0)
-    field_step(1)
-    got_rows = xin.at[pl.ds(0, N_VOX - 1)]
-    pltpu.make_async_copy(got_rows, got_rows, xr_sem).wait()
+    field_step(0)
+    lax.fori_loop(1, N_VOX, pass_half, 0)
+    got_beside = xin.at[pl.ds(0, N_VOX - 1), beside_rows]
+    got_halves = xin.at[pl.ds(0, N_VOX - 1), pl.ds(0, part_rows)]
+    pltpu.make_async_copy(got_beside, got_beside, xr_sem).wait()
+    pltpu.make_async_copy(got_halves, got_halves, cr_sem).wait()
 
     n_here = N_VOX * ROWS
     extra = xin[:, slots : slots + ROWS, :].astype(jnp.float32).reshape(n_here, width).T
     per = width // groups
     low = (lax.broadcasted_iota(jnp.int32, (n_here, width), 0) & (ROWS - 1)) < CAP
-    sums = jnp.zeros((2 * j_dev, members), jnp.float32)
+    u = z % 2 * NC + core
+    share = SIDE // QUAD
+    n_side = members // SIDE
+    sums = jnp.zeros((n_side * share + j_dev, members), jnp.float32)
     lanes = jnp.zeros(TILE, jnp.float32)
     pair = 2 * width
     contract = (((1,), (1,)), ((), ()))
@@ -232,7 +259,11 @@
         own_pred = pred_ref[pl.ds(pl.multiple_of(g * j_dev, 8), j_dev), :]
         misfit = (seen - own_pred) * inv_noise + extra[per * q : per * q + j_dev]
         misfit = misfit.astype(jnp.bfloat16).astype(jnp.float32)
-        left = jnp.concatenate([(own_pred - centre) * scale, misfit], axis=0).astype(jnp.bfloat16)
+        some = [
+            pred_ref[pl.ds(pl.multiple_of(side * SIDE + u * share, 8), share), :] for side in range(n_side)
+        ]
+        left = jnp.concatenate([(p - centre) * scale for p in some] + [misfit], axis=0)
+        left = left.astype(jnp.bfloat16)
         sums = sums + lax.dot_general(left, scaled, contract, preferred_element_type=jnp.float32)
         squares = misfit * misfit
         for i in range(j_dev // 8):
@@ -240,14 +271,21 @@
                 lanes = lanes + squares[8 * i : 8 * i + 8, 128 * c : 128 * c + 128]
 
     n_row, n_col = j_dev // 8, members // 128
-    n_gram = n_row * n_col
-    n_tiles = 2 * n_gram + 1
-    for h in range(2):
-        for i in range(n_row):
-            for c in range(n_col):
-                t = h * (n_gram + 1) + i * n_col + c
-                part[t] = sums[h * j_dev + 8 * i : h * j_dev + 8 * i + 8, 128 * c : 128 * c + 128]
-    part[n_gram] = lanes
+    strips_u = share // 8
+    gram_at = [(side, strip, (side + turn) % n_side)
+               for side in range(n_side) for strip in range(strips_u) for turn in range(2)]
+    tiles = [sums[side * share + 8 * strip : side * share + 8 * strip + 8, SIDE * k : SIDE * (k + 1)]
+             for side, strip, k in gram_at]
+    n_gram = len(tiles)
+    n_pieces = n_gram // 2
+    tiles.append(lanes)
+    first_cross = n_side * share
+    for i in range(n_row):
+        for c in range(n_col):
+            tiles.append(sums[first_cross + 8 * i : first_cross + 8 * i + 8, 128 * c : 128 * c + 128])
+    for t, tile in enumerate(tiles):
+        part[t // 2, t % 2 * 8 : t % 2 * 8 + 8] = tile
+    n_tiles = len(tiles) // 2
 
     def send_part(i, _):
         t = (v + i) % n_tiles
@@ -259,7 +297,7 @@
         return 0
 
     lax.fori_loop(0, n_tiles, send_part, 0)
-    field_step(2)
+    field_step(1)
 
     @pl.when(v < n_tiles)
     def _():
@@ -281,49 +319,51 @@
         whole = tot.at[pl.ds(0, n_tiles)]
         pltpu.make_async_copy(whole, whole, ar_sem).wait()
 
-    gbuf[g] = tot[0 : n_gram + 1]
-
-    def rows_copy(i, arriving):
-        slot = gbuf.at[((z + NZ - i) % NZ) * NC + core if arriving else g]
-        return remote(slot, slot, gs_sem.at[i], gr_sem.at[i], {"grp": z_peer(i)})
-
-    def rows_partner(i, arriving):
-        slot = gbuf.at[((z + NZ - i) % NZ) * NC + (1 - core if arriving else core)]
-        return remote(slot, slot, gps_sem.at[i], gpr_sem.at[i], {"grp": partner})
-
-    def rows_send(i, _):
-        rows_copy(i, False).start()
-        return 0
-
-    def rows_forward(i, _):
-        rows_copy(i, True).wait_recv()
-        rows_partner(i, False).start()
-        return 0
-
-    def rows_from(i, _):
-        rows_partner(i, True).wait_recv()
-        return 0
-
-    lax.fori_loop(1, NZ, rows_send, 0)
-    rows_partner(0, False).start()
+    gbuf[u] = tot[0:n_pieces]
+    mbuf[z] = tot[n_pieces, 0:8]
+    beyond = {"grp": (z + 1 - z % 2 * 2) * NC + core}
+    u_beyond = (1 - z % 2) * NC + core
+
+    def gram_copy(n, slot, to):
+        return remote(gbuf.at[slot], gbuf.at[slot], gs_sem.at[n], gr_sem.at[n], to)
+
+    def squares_copy(i, arriving):
+        slot = mbuf.at[(z + NZ - i) % NZ if arriving else z]
+        return remote(slot, slot, ms_sem.at[i], mr_sem.at[i], {"grp": z_peer(i)})
+
+    gram_copy(0, u, beyond).start()
+    gram_copy(1, u, {"grp": partner}).start()
+
+    def squares_send(i, _):
+        squares_copy(i, False).start()
+        return 0
+
+    lax.fori_loop(1, NZ, squares_send, 0)
+    field_step(2)
     for i in range(n_row):
         for c in range(n_col):
-            cross_ref[8 * i : 8 * i + 8, 128 * c : 128 * c + 128] = tot[n_gram + 1 + i * n_col + c]
-    lax.fori_loop(1, NZ, rows_forward, 0)
-    lax.fori_loop(0, NZ, rows_from, 0)
-
-    def place(n, _):
-        for i in range(n_row):
-            row = pl.multiple_of(n * j_dev + 8 * i, 8)
-            for c in range(n_col):
-                gram_ref[pl.ds(row, 8), 128 * c : 128 * c + 128] = gbuf[n, i * n_col + c]
-        return 0
-
-    lax.fori_loop(0, N_GRP, place, 0)
-    squares_all = jnp.sum(gbuf[:, n_gram], axis=0)
-    damping = jnp.sum(squares_all, keepdims=True) * (1.0 / (members * n_obs * N_VOX))
-    field_step(3)
-    weights = solve(gram_ref, cross_ref, damping, lambda: field_step(z_last)).astype(jnp.bfloat16)
+            t = n_gram + 1 + i * n_col + c
+            cross_ref[8 * i : 8 * i + 8, 128 * c : 128 * c + 128] = tot[t // 2, t % 2 * 8 : t % 2 * 8 + 8]
+    gram_copy(0, u_beyond, beyond).wait_recv()
+    gram_copy(2, u_beyond, {"grp": partner}).start()
+
+    def squares_wait(i, _):
+        squares_copy(i, True).wait_recv()
+        return 0
+
+    lax.fori_loop(1, NZ, squares_wait, 0)
+    msum[core] = jnp.sum(mbuf[...], axis=0)
+    squares_across = remote(msum.at[core], msum.at[core], mps_sem, mpr_sem, {"grp": partner})
+    squares_across.start()
+    gram_copy(1, z % 2 * NC + 1 - core, {"grp": partner}).wait_recv()
+    gram_copy(2, (1 - z % 2) * NC + 1 - core, {"grp": partner}).wait_recv()
+    for n in range(QUAD):
+        for t, (side, strip, k) in enumerate(gram_at):
+            row = side * SIDE + n * share + 8 * strip
+            gram_ref[row : row + 8, SIDE * k : SIDE * (k + 1)] = gbuf[n, t // 2, t % 2 * 8 : t % 2 * 8 + 8]
+    remote(msum.at[1 - core], msum.at[1 - core], mps_sem, mpr_sem, {"grp": partner}).wait_recv()
+    damping = jnp.sum(msum[0] + msum[1], keepdims=True) * (1.0 / (members * n_obs * N_VOX))
+    weights = solve(gram_ref, cross_ref, damping, field_step).astype(jnp.bfloat16)
 
     def field_from(i, _):
         field_partner(i, True).wait_recv()
@@ -351,21 +391,24 @@
             cols = slice(h * lane_half + n * piece, h * lane_half + (n + 1) * piece)
             out_ref[:, cols] = mixture[h * j_dev : (h + 1) * j_dev]
 
-    sent_rows = xout.at[pl.ds(0, N_VOX - 1)]
-    pltpu.make_async_copy(sent_rows, sent_rows, xs_sem).wait()
-
+    pltpu.make_async_copy(got_beside, got_beside, xs_sem).wait()
+    pltpu.make_async_copy(got_halves, got_halves, hs_sem).wait()
+    pltpu.make_async_copy(got_halves, got_halves, cs_sem).wait()
     def grp_sent(i, _):
         peer_copy(i, False).wait_send()
-        rows_copy(i, False).wait_send()
+        squares_copy(i, False).wait_send()
         return 0
 
     def partner_sent(i, _):
-        for copy in (partner_copy(i, False), rows_partner(i, False), field_partner(i, False)):
+        for copy in (partner_copy(i, False), field_partner(i, False)):
             copy.wait_send()
         return 0
 
     lax.fori_loop(1, NZ, grp_sent, 0)
     lax.fori_loop(0, NZ, partner_sent, 0)
+    for n in range(3):
+        gram_copy(n, u, {"grp": partner}).wait_send()
+    squares_across.wait_send()
     for way in range(2):
         for step in range(1, z_last + 1):
             field_copy(way, step, False).wait_send()
@@ -389,8 +432,8 @@
     blocks_dev = vox_dev // block_vox
     n_obs = sensitivity.shape[0]
     members = j_dev * N_GRP
-    n_gram = (j_dev // 8) * (members // 128)
-    n_tiles = 2 * n_gram + 1
+    n_gram = (members // SIDE) * (SIDE // QUAD // 8) * 2
+    n_tiles = (n_gram + 1 + (j_dev // 8) * (members // 128)) // 2
     f32, bf16 = jnp.float32, jnp.bfloat16
     dma = pltpu.SemaphoreType.DMA
     vmem = pl.BlockSpec(memory_space=pltpu.VMEM)
@@ -414,13 +457,15 @@
             pltpu.VMEM((N_GRP, 2 * j_dev, blocks_dev * width // 2), bf16),
             pltpu.VMEM((members, blocks_dev * width), bf16),
             pltpu.VMEM((members, N_VOX * ROWS), f32),
-            pltpu.VMEM((n_tiles, *TILE), f32),
-            pltpu.VMEM((N_VOX, *TILE), f32),
-            pltpu.VMEM((n_tiles, *TILE), f32),
-            pltpu.VMEM((N_GRP, n_gram + 1, *TILE), f32),
-            dma, dma, dma((NZ,)), dma((NZ,)), dma((NZ,)), dma((NZ,)),
+            pltpu.VMEM((n_tiles, *PIECE), f32),
+            pltpu.VMEM((N_VOX, *PIECE), f32),
+            pltpu.VMEM((n_tiles, *PIECE), f32),
+            pltpu.VMEM((QUAD, n_gram // 2, *PIECE), f32),
+            pltpu.VMEM((NZ, *TILE), f32),
+            pltpu.VMEM((NC, *TILE), f32),
+            dma, dma, dma, dma((N_VOX,)), dma, dma, dma((NZ,)), dma((NZ,)), dma((NZ,)), dma((NZ,)),
             dma, dma, dma, dma,
-            dma((NZ,)), dma((NZ,)), dma((NZ,)), dma((NZ,)),
+            dma((3,)), dma((3,)), dma((NZ,)), dma((NZ,)), dma, dma,
             dma((2, NZ // 2)), dma((2, NZ // 2)), dma((NZ,)), dma((NZ,)),
         ],
         compiler_params=pltpu.CompilerParams(
@@ -474,22 +519,23 @@
         return found + jnp.where(eye, damp, 0.0) if i == j else found
 
     c0, c1, c2 = (cross_ref[:, i * b : (i + 1) * b] for i in range(3))
-    a01, a02, a12 = block(0, 1), block(0, 2), block(1, 2)
-    a10, a20, a21 = block(1, 0), block(2, 0), block(2, 1)
+    a01, a12, a20 = block(0, 1), block(1, 2), block(2, 0)
+    a10, a02 = a01.T, a20.T
     i0 = inverse(block(0, 0), PIVOTS)
+    between(3)
     u01 = product(i0, a01)
     u02 = product(i0, a02)
     y0 = product(c0, i0)
     i1 = inverse(block(1, 1) - product(a10, u01), PIVOTS)
     a12 = a12 - product(a10, u02)
-    a21 = a21 - product(a20, u01)
+    a21 = a12.T
     a22 = block(2, 2) - product(a20, u02)
     z1 = c1 - product(y0, a01)
     z2 = c2 - product(y0, a02)
-    between()
     u12 = product(i1, a12)
     y1 = product(z1, i1)
     i2 = inverse(a22 - product(a21, u12), PIVOTS)
+    between(NZ // 2)
     z2 = z2 - product(y1, a12)
     x2 = product(z2, i2)
     x1 = product(z1 - product(x2, a21), i1)

time: 86.5 us -> 87.7 us (1.014)
  Pallas kernels: 84.2 us -> 85.4 us
    pallas_call x1, Pallas kernels: 84.2 us -> 85.4 us  [update(): pl.pallas_call(update_kernel, out_shape=jax.ShapeDtypeStruct((j_dev, vox_...]
where the time goes in v3:
time: 87.7 us; the launch traced here: 87.5 us
  Pallas kernels  85.4 us (97%)
  other arithmetic  2.09 us (2%)
    pallas_call x1, Pallas kernels, update(): pl.pallas_call(update_kernel, out_shape=jax.ShapeDtypeStruct((j_dev, vox_...  85.4 us
    add x1, other arithmetic, on_device(): log_modulus + update(log_modulus, basis, sensitivity, obs_block.reshape(1...  2.09 us

profile of v3, /device:TPU:1, one launch (start us, length us, event | category | flops | bytes accessed | tf_op | source)
XLA Modules:
  0.0 87.5 jit_solution(15079775268234386534)
XLA Ops:
  0.0 0.0 copy-start
  0.0 85.4 %update.1 = f32[24,8192]{1,0:T(8,128)} custom-call(f32[24,8192]{1,0:T(8,128)} %lm_hbm.1, bf16[1024,128]{1,0:T(8,128)(2,1)} %basis_hbm.1, bf16[1024,128]{1,0:T(8,128)(2,1)} %sens_hbm.1, s32[1,1024]{1,0:T(1,128)} %bitcast.3, f32[1,1024]{1,0:T(1,128)} %bitcast.4, f32[1,1024]{1,0:T(1,128)} %bitcast.5, f32[24,1024]{1,0:T(8,128)} %pert_hbm.1), custom_call_target="tpu_custom_call" | custom-call | tf_op jit(solution)/shard_map/update/pallas_call | solution.py:441
  85.4 0.0 copy-done
  85.4 2.1 %add.3 = f32[24,8192]{1,0:T(8,128)} add(f32[24,8192]{1,0:T(8,128)S(1)} %copy-done, f32[24,8192]{1,0:T(8,128)} %update.1) | non-fusion elementwise | flops 196608 | bytes 2359296 | tf_op jit(solution)/shard_map/add | solution.py:548
Async XLA Ops:
  0.0 85.4 %copy-start = (f32[24,8192]{1,0:T(8,128)S(1)}, f32[24,8192]{1,0:T(8,128)}, u32[]{:S(2)}) copy-start(f32[24,8192]{1,0:T(8,128)} %lm_hbm.1) | copy-start | bytes 2359300

commit v4 on v3

--- a/solution.py
+++ b/solution.py
@@ -210,6 +210,7 @@
     xin[v] = xout[v]
     lm = lm_ref[...]
     abuf[g] = jnp.concatenate([lm[:, :lane_half], lm[:, lane_half:]], axis=0).astype(jnp.bfloat16)
+    field_step(0)
     lax.fori_loop(1, NZ, forward, 0)
     lax.fori_loop(0, NZ, from_partner, 0)
 
@@ -224,8 +225,8 @@
         return 0
 
     lax.fori_loop(0, NZ, place_pair, 0)
-    field_step(0)
     lax.fori_loop(1, N_VOX, pass_half, 0)
+    field_step(1)
     got_beside = xin.at[pl.ds(0, N_VOX - 1), beside_rows]
     got_halves = xin.at[pl.ds(0, N_VOX - 1), pl.ds(0, part_rows)]
     pltpu.make_async_copy(got_beside, got_beside, xr_sem).wait()
@@ -297,7 +298,7 @@
         return 0
 
     lax.fori_loop(0, n_tiles, send_part, 0)
-    field_step(1)
+    field_step(2)
 
     @pl.when(v < n_tiles)
     def _():
@@ -339,7 +340,6 @@
         return 0
 
     lax.fori_loop(1, NZ, squares_send, 0)
-    field_step(2)
     for i in range(n_row):
         for c in range(n_col):
             t = n_gram + 1 + i * n_col + c
@@ -363,6 +363,7 @@
             gram_ref[row : row + 8, SIDE * k : SIDE * (k + 1)] = gbuf[n, t // 2, t % 2 * 8 : t % 2 * 8 + 8]
     remote(msum.at[1 - core], msum.at[1 - core], mps_sem, mpr_sem, {"grp": partner}).wait_recv()
     damping = jnp.sum(msum[0] + msum[1], keepdims=True) * (1.0 / (members * n_obs * N_VOX))
+    field_step(3)
     weights = solve(gram_ref, cross_ref, damping, field_step).astype(jnp.bfloat16)
 
     def field_from(i, _):
@@ -522,7 +523,6 @@
     a01, a12, a20 = block(0, 1), block(1, 2), block(2, 0)
     a10, a02 = a01.T, a20.T
     i0 = inverse(block(0, 0), PIVOTS)
-    between(3)
     u01 = product(i0, a01)
     u02 = product(i0, a02)
     y0 = product(c0, i0)
@@ -534,8 +534,8 @@
     z2 = c2 - product(y0, a02)
     u12 = product(i1, a12)
     y1 = product(z1, i1)
+    between(NZ // 2)
     i2 = inverse(a22 - product(a21, u12), PIVOTS)
-    between(NZ // 2)
     z2 = z2 - product(y1, a12)
     x2 = product(z2, i2)
     x1 = product(z1 - product(x2, a21), i1)

time: 87.7 us -> 83.4 us (0.951)
  Pallas kernels: 85.4 us -> 81.1 us
    pallas_call x1, Pallas kernels: 85.4 us -> 81.1 us  [update(): pl.pallas_call(update_kernel, out_shape=jax.ShapeDtypeStruct((j_dev, vox_...]
where the time goes in v4:
time: 83.4 us; the launch traced here: 83.3 us
  Pallas kernels  81.1 us (97%)
  other arithmetic  2.09 us (3%)
    pallas_call x1, Pallas kernels, update(): pl.pallas_call(update_kernel, out_shape=jax.ShapeDtypeStruct((j_dev, vox_...  81.1 us
    add x1, other arithmetic, on_device(): log_modulus + update(log_modulus, basis, sensitivity, obs_block.reshape(1...  2.09 us

profile of v4, /device:TPU:1, one launch (start us, length us, event | category | flops | bytes accessed | tf_op | source)
XLA Modules:
  0.0 83.3 jit_solution(11973807041072804798)
XLA Ops:
  0.0 0.0 copy-start
  0.0 81.1 %update.1 = f32[24,8192]{1,0:T(8,128)} custom-call(f32[24,8192]{1,0:T(8,128)} %lm_hbm.1, bf16[1024,128]{1,0:T(8,128)(2,1)} %basis_hbm.1, bf16[1024,128]{1,0:T(8,128)(2,1)} %sens_hbm.1, s32[1,1024]{1,0:T(1,128)} %bitcast.3, f32[1,1024]{1,0:T(1,128)} %bitcast.4, f32[1,1024]{1,0:T(1,128)} %bitcast.5, f32[24,1024]{1,0:T(8,128)} %pert_hbm.1), custom_call_target="tpu_custom_call" | custom-call | tf_op jit(solution)/shard_map/update/pallas_call | solution.py:442
  81.2 0.0 copy-done
  81.2 2.1 %add.3 = f32[24,8192]{1,0:T(8,128)} add(f32[24,8192]{1,0:T(8,128)S(1)} %copy-done, f32[24,8192]{1,0:T(8,128)} %update.1) | non-fusion elementwise | flops 196608 | bytes 2359296 | tf_op jit(solution)/shard_map/add | solution.py:548
Async XLA Ops:
  0.0 81.2 %copy-start = (f32[24,8192]{1,0:T(8,128)S(1)}, f32[24,8192]{1,0:T(8,128)}, u32[]{:S(2)}) copy-start(f32[24,8192]{1,0:T(8,128)} %lm_hbm.1) | copy-start | bytes 2359300

commit v5 on v4

--- a/solution.py
+++ b/solution.py
@@ -140,6 +140,10 @@
             field_partner(step, False).start()
             field_partner(NZ - step, False).start()
 
+    lm = lm_ref[...]
+    abuf[g] = jnp.concatenate([lm[:, :lane_half], lm[:, lane_half:]], axis=0).astype(jnp.bfloat16)
+    field_step(0)
+
     n_blocks = blocks_dev * N_VOX
     slots = blocks_dev * CAP
     groups = slots // ROWS
@@ -208,9 +212,6 @@
 
     lax.fori_loop(1, N_VOX, send_rows, 0)
     xin[v] = xout[v]
-    lm = lm_ref[...]
-    abuf[g] = jnp.concatenate([lm[:, :lane_half], lm[:, lane_half:]], axis=0).astype(jnp.bfloat16)
-    field_step(0)
     lax.fori_loop(1, NZ, forward, 0)
     lax.fori_loop(0, NZ, from_partner, 0)
 
@@ -298,7 +299,6 @@
         return 0
 
     lax.fori_loop(0, n_tiles, send_part, 0)
-    field_step(2)
 
     @pl.when(v < n_tiles)
     def _():
@@ -312,6 +312,11 @@
             return 0
 
         lax.fori_loop(1, N_VOX, spread, 0)
+
+    field_step(2)
+
+    @pl.when(v < n_tiles)
+    def _():
         most = tot.at[pl.ds(0, n_tiles - 1)]
         pltpu.make_async_copy(most, most, ar_sem).wait()
 

time: 83.4 us -> 82.9 us (level)
  no operation moved by 1% of the time
where the time goes in v5:
time: 82.9 us; the launch traced here: 82.7 us
  Pallas kernels  80.6 us (97%)
  other arithmetic  2.09 us (3%)
    pallas_call x1, Pallas kernels, update(): pl.pallas_call(update_kernel, out_shape=jax.ShapeDtypeStruct((j_dev, vox_...  80.6 us
    add x1, other arithmetic, on_device(): log_modulus + update(log_modulus, basis, sensitivity, obs_block.reshape(1...  2.09 us

profile of v5, /device:TPU:1, one launch (start us, length us, event | category | flops | bytes accessed | tf_op | source)
XLA Modules:
  0.0 82.7 jit_solution(9878961870461209290)
XLA Ops:
  0.0 0.0 copy-start
  0.0 80.6 %update.1 = f32[24,8192]{1,0:T(8,128)} custom-call(f32[24,8192]{1,0:T(8,128)} %lm_hbm.1, bf16[1024,128]{1,0:T(8,128)(2,1)} %basis_hbm.1, bf16[1024,128]{1,0:T(8,128)(2,1)} %sens_hbm.1, s32[1,1024]{1,0:T(1,128)} %bitcast.3, f32[1,1024]{1,0:T(1,128)} %bitcast.4, f32[1,1024]{1,0:T(1,128)} %bitcast.5, f32[24,1024]{1,0:T(8,128)} %pert_hbm.1), custom_call_target="tpu_custom_call" | custom-call | tf_op jit(solution)/shard_map/update/pallas_call | solution.py:447
  80.6 0.0 copy-done
  80.6 2.1 %add.3 = f32[24,8192]{1,0:T(8,128)} add(f32[24,8192]{1,0:T(8,128)S(1)} %copy-done, f32[24,8192]{1,0:T(8,128)} %update.1) | non-fusion elementwise | flops 196608 | bytes 2359296 | tf_op jit(solution)/shard_map/add | solution.py:553
Async XLA Ops:
  0.0 80.6 %copy-start = (f32[24,8192]{1,0:T(8,128)S(1)}, f32[24,8192]{1,0:T(8,128)}, u32[]{:S(2)}) copy-start(f32[24,8192]{1,0:T(8,128)} %lm_hbm.1) | copy-start | bytes 2359300
